TPU v7x, 512 devices: a whole 4x8x8 slice. The times are simulated.
512 devices in a mesh: pair: 128 (over x_hi, y, z), row: 4 (over x_lo, core).
Axes of the slice: x: 4 (x_hi: 2, x_lo: 2; x = x_hi * 2 + x_lo), y: 8, z: 8, core: 2. Of those that a mesh axis runs over, the one named last changes fastest.
Arguments:
- statistic: bfloat16 [16384, 16384], P('row', 'pair'), may hold values from -1 to 12, as said below
- initial_basis: bfloat16 [16384, 16384], P('row', 'pair'), may hold values from -6 to 6
- moving_slot: int32 [4, 128], P(None, 'pair'), may hold values from 0 to 1
Outputs:
- eigvectors: float32 [16384, 16384], P('row', 'pair')
- spectrum: float32 [16384], P('pair')
- off_ratio: float32 [4], replicated
Inputs may be any that keep to these rules, and one draw needn't show every extreme that they name: `statistic`: symmetric and positive definite. `moving_slot`: which of a pair's two blocks moves on.
All inputs are finite; a program needn't handle non-finite values.
Results may differ from a plain program's by a relative error of at most 0.0003.
Values sent between devices are 32-bit elements; how exact they have to be, the bound alone decides.
No kernel may reach another device: no remote copies, remote signals or barrier semaphores. Data moves between devices by JAX's collectives and lax.ppermute only.
A program may use at most 64 MiB of HBM per device.

v0:
```python
import jax
import jax.numpy as jnp
from jax import lax
from jax.sharding import PartitionSpec as P

ROUNDS = 4
HIGH = lax.Precision.HIGHEST


def from_behind(value, axis, steps):
    count = lax.axis_size(axis)
    pairs = [(source, (source + steps) % count) for source in range(count)]
    return lax.ppermute(value, axis, pairs)


def product(left, right):
    return jnp.dot(left, right, precision=HIGH, preferred_element_type=jnp.float32)


def inner_product(left, right):
    return lax.dot_general(
        left, right, (((0,), (0,)), ((), ())), precision=HIGH, preferred_element_type=jnp.float32
    )


def orthonormal(block):
    square = inner_product(block, block)
    lower = jnp.linalg.cholesky(square)
    return jax.scipy.linalg.solve_triangular(lower, block.T, lower=True).T


def rotation(gram):
    basis = orthonormal(gram)
    basis = orthonormal(product(gram, basis))
    return basis


def full_gram(factor):
    return lax.psum(inner_product(factor, factor), "row")


def on_device(statistic, initial_basis, moving_slot):
    rows, width = statistic.shape
    half = width // 2
    vectors = initial_basis.astype(jnp.float32)
    factor = statistic.astype(jnp.float32)
    mask = jnp.eye(width, dtype=bool)
    gram = full_gram(factor)
    ratios = []
    for step in range(ROUNDS):
        squares = gram * gram
        off_part = jnp.sum(jnp.where(mask, jnp.float32(0.0), squares))
        diag_part = jnp.sum(jnp.where(mask, squares, jnp.float32(0.0)))
        off_total, diag_total = lax.psum((off_part, diag_part), "pair")
        ratios.append(jnp.sqrt(off_total / diag_total))
        basis = rotation(gram)
        factor = product(factor, basis)
        vectors = product(vectors, basis)
        first_leaves = moving_slot[step, 0] == 0
        leaving = jnp.where(
            first_leaves,
            jnp.concatenate([factor[:, :half], vectors[:, :half]], axis=1),
            jnp.concatenate([factor[:, half:], vectors[:, half:]], axis=1),
        )
        stay_factor = jnp.where(first_leaves, factor[:, half:], factor[:, :half])
        stay_vectors = jnp.where(first_leaves, vectors[:, half:], vectors[:, :half])
        arrived = from_behind(leaving, "pair", 1)
        come_factor = arrived[:, :half]
        come_vectors = arrived[:, half:]
        factor = jnp.where(
            first_leaves,
            jnp.concatenate([come_factor, stay_factor], axis=1),
            jnp.concatenate([stay_factor, come_factor], axis=1),
        )
        vectors = jnp.where(
            first_leaves,
            jnp.concatenate([come_vectors, stay_vectors], axis=1),
            jnp.concatenate([stay_vectors, come_vectors], axis=1),
        )
        if step + 1 < ROUNDS:
            gram = full_gram(factor)
    off_ratio = jnp.stack(ratios)
    column_sq = lax.psum(jnp.sum(factor * factor, axis=0), "row")
    spectrum = jnp.sqrt(column_sq)
    return (vectors, spectrum, off_ratio)


def solution(mesh):
    return jax.shard_map(
        on_device,
        mesh=mesh,
        in_specs=(P("row", "pair"), P("row", "pair"), P(None, "pair")),
        out_specs=(P("row", "pair"), P("pair"), P()),
        check_vma=False,
    )
```

profile of v0, /device:TPU:1, one launch (start us, length us, event | category | flops | bytes accessed | tf_op | source)
XLA Modules:
  0.0 1018.9 jit_solution(724183624023404392)
XLA Ops:
  7.2 1.2 copy-done
  10.9 52.7 %all-reduce.6.cloned.1.call-done = f32[128,128]{1,0:T(8,128)} async-done(((f32[128,128]{1,0:T(8,128)}), f32[128,128]{1,0:T(8,128)}) %all-reduce.6.cloned.1.call-update) | async-done | bytes 65552 | tf_op jit(solution)/shard_map/psum | solution.py:39
  63.6 1.2 fusion.112
  64.9 11.7 %cholesky.134 = f32[128,128]{1,0:T(8,128)S(1)} custom-call(f32[128,128]{1,0:T(8,128)S(1)} %fusion.74), custom_call_target="Cholesky" | custom-call | tf_op jit(solution)/shard_map/jit(cholesky)/cholesky | solution.py:28
  78.0 9.8 custom-call.12
  90.4 11.7 %cholesky.145 = f32[128,128]{1,0:T(8,128)S(1)} custom-call(f32[128,128]{1,0:T(8,128)S(1)} %fusion.70), custom_call_target="Cholesky" | custom-call | tf_op jit(solution)/shard_map/jit(cholesky)/cholesky | solution.py:28
  103.5 10.1 custom-call.13
  116.8 3.2 collective-permute-start
  120.0 52.6 %collective-permute-done = f32[4096,128]{0,1:T(8,128)S(1)} collective-permute-done((f32[4096,128]{0,1:T(8,128)S(1)}, f32[4096,128]{0,1:T(8,128)S(1)}, u32[]{:S(2)}, u32[]{:S(2)}) %collective-permute-start) | collective-permute-done | bytes 2097184 | tf_op jit(solution)/shard_map/ppermute | solution.py:13
  172.8 2.6 fusion.25
  176.1 41.7 %all-reduce.8.cloned.1.call-done = f32[128,128]{1,0:T(8,128)} async-done(((f32[128,128]{1,0:T(8,128)}), f32[128,128]{1,0:T(8,128)}) %all-reduce.8.cloned.1.call-update) | async-done | bytes 65552 | tf_op jit(solution)/shard_map/psum | solution.py:39
  217.8 1.2 fusion.115
  219.1 11.7 %cholesky.156 = f32[128,128]{1,0:T(8,128)S(1)} custom-call(f32[128,128]{1,0:T(8,128)S(1)} %fusion.66), custom_call_target="Cholesky" | custom-call | tf_op jit(solution)/shard_map/jit(cholesky)/cholesky | solution.py:28
  232.2 9.8 custom-call.14
  244.6 11.7 %cholesky.167 = f32[128,128]{1,0:T(8,128)S(1)} custom-call(f32[128,128]{1,0:T(8,128)S(1)} %fusion.62), custom_call_target="Cholesky" | custom-call | tf_op jit(solution)/shard_map/jit(cholesky)/cholesky | solution.py:28
  257.7 9.9 custom-call.15
  267.9 3.8 fusion.24
  271.8 2.1 fusion
  274.8 3.2 collective-permute-start.1
  278.0 52.6 %collective-permute-done.1 = f32[4096,128]{0,1:T(8,128)S(1)} collective-permute-done((f32[4096,128]{0,1:T(8,128)S(1)}, f32[4096,128]{0,1:T(8,128)S(1)}, u32[]{:S(2)}, u32[]{:S(2)}) %collective-permute-start.1) | collective-permute-done | bytes 2097184 | tf_op jit(solution)/shard_map/ppermute | solution.py:13
  331.8 2.6 fusion.23
  335.5 41.2 %all-reduce.10.cloned.1.call-done = f32[128,128]{1,0:T(8,128)} async-done(((f32[128,128]{1,0:T(8,128)}), f32[128,128]{1,0:T(8,128)}) %all-reduce.10.cloned.1.call-update) | async-done | bytes 65552 | tf_op jit(solution)/shard_map/psum | solution.py:39
  376.7 1.2 fusion.118
  378.0 11.7 %cholesky.178 = f32[128,128]{1,0:T(8,128)S(1)} custom-call(f32[128,128]{1,0:T(8,128)S(1)} %fusion.58), custom_call_target="Cholesky" | custom-call | tf_op jit(solution)/shard_map/jit(cholesky)/cholesky | solution.py:28
  391.1 9.8 custom-call.16
  400.9 1.1 fusion.55
  403.6 11.7 %cholesky.189 = f32[128,128]{1,0:T(8,128)S(1)} custom-call(f32[128,128]{1,0:T(8,128)S(1)} %fusion.54), custom_call_target="Cholesky" | custom-call | tf_op jit(solution)/shard_map/jit(cholesky)/cholesky | solution.py:28
  416.6 9.9 custom-call.17
  426.9 3.8 fusion.22
  430.7 2.1 fusion.6
  433.8 3.2 collective-permute-start.2
  437.0 52.6 %collective-permute-done.2 = f32[4096,128]{0,1:T(8,128)S(1)} collective-permute-done((f32[4096,128]{0,1:T(8,128)S(1)}, f32[4096,128]{0,1:T(8,128)S(1)}, u32[]{:S(2)}, u32[]{:S(2)}) %collective-permute-start.2) | collective-permute-done | bytes 2097184 | tf_op jit(solution)/shard_map/ppermute | solution.py:13
  490.7 2.6 fusion.21
  494.0 41.7 %all-reduce.12.cloned.1.call-done = f32[128,128]{1,0:T(8,128)} async-done(((f32[128,128]{1,0:T(8,128)}), f32[128,128]{1,0:T(8,128)}) %all-reduce.12.cloned.1.call-update) | async-done | bytes 65552 | tf_op jit(solution)/shard_map/psum | solution.py:39
  535.7 1.2 fusion.121
  537.0 11.7 %cholesky.200 = f32[128,128]{1,0:T(8,128)S(1)} custom-call(f32[128,128]{1,0:T(8,128)S(1)} %fusion.50), custom_call_target="Cholesky" | custom-call | tf_op jit(solution)/shard_map/jit(cholesky)/cholesky | solution.py:28
  550.0 9.8 custom-call.18
  562.5 11.9 %cholesky.211 = f32[128,128]{1,0:T(8,128)S(1)} custom-call(f32[128,128]{1,0:T(8,128)S(1)} %fusion.46), custom_call_target="Cholesky" | custom-call | tf_op jit(solution)/shard_map/jit(cholesky)/cholesky | solution.py:28
  575.7 9.8 custom-call.19
  585.8 3.8 fusion.20
  589.7 2.1 fusion.12
  591.8 1.3 broadcast_select_fusion
  593.7 3.2 collective-permute-start.3
  599.6 339.6 %all-reduce = (f32[]{:T(128)}, f32[]{:T(128)}, f32[]{:T(128)}, f32[]{:T(128)}, f32[]{:T(128)}, /*index=5*/f32[]{:T(128)}, f32[]{:T(128)}, f32[]{:T(128)}) all-reduce(f32[]{:T(128)} %get-tuple-element.15, f32[]{:T(128)} %get-tuple-element.14, f32[]{:T(128)} %get-tuple-element.13, ...), channel_id=1, replica_groups=mesh['pair'=128,'row'=4] {'pair'}, use_global_device_ids=true, to_apply=%region_21.24 | all-reduce | flops 8 | bytes 64 | tf_op jit(solution)/shard_map/psum | solution.py:54
  945.0 2.7 fusion.102
  947.9 1.8 copy.14
  949.7 2.5 fusion.19
  952.2 59.3 %psum.95 = f32[128]{0:T(128)S(1)} all-reduce(f32[128]{0:T(128)S(1)} %fusion.19), channel_id=1, replica_groups=mesh['pair'=128,'row'=4] {'row'}, use_global_device_ids=true, to_apply=%region_7.10 | all-reduce | flops 128 | bytes 1024 | tf_op jit(solution)/shard_map/psum | solution.py:83
  (109 shorter events, 35.7 us)
Async XLA Ops:
  7.2 1.2 copy-start
  7.2 2.4 copy-start.10
  7.2 56.4 %all-reduce.6.cloned.1.call-start = ((), (), s32[]{:S(2)}) async-start(), calls=%async_computation | async-start | bytes 131072 | tf_op jit(solution)/shard_map/psum | solution.py:39
  9.5 208.3 %all-reduce.8.cloned.1.call-start = ((), (), s32[]{:S(2)}) async-start(), calls=%async_computation.1 | async-start | bytes 131072 | tf_op jit(solution)/shard_map/psum | solution.py:39
  90.0 24.9 %copy-start.9 = (bf16[4096,128]{1,0:T(8,128)(2,1)S(1)}, bf16[4096,128]{1,0:T(8,128)(2,1)}, u32[]{:S(2)}) copy-start(bf16[4096,128]{1,0:T(8,128)(2,1)} %param.7) | copy-start | bytes 3145732
  116.5 56.3 %copy-start.4 = (f32[4096,64]{0,1:T(8,128)}, f32[4096,64]{0,1:T(8,128)S(1)}, u32[]{:S(2)}) copy-start(f32[4096,64]{0,1:T(8,128)S(1)} %get-tuple-element.61) | copy-start | bytes 3145732
  116.8 55.8 %collective-permute-start = (f32[4096,128]{0,1:T(8,128)S(1)}, f32[4096,128]{0,1:T(8,128)S(1)}, u32[]{:S(2)}, u32[]{:S(2)}) collective-permute-start(f32[4096,128]{0,1:T(8,128)S(1)} %maximum_select_fusion), channel_id=1, source_target_pairs={{0,4},{4,8},{8,12},{12,16},{16,20},{20,24},{24,28},{28,32},{32,36}... | collective-permute-start | bytes 6291464 | tf_op jit(solution)/shard_map/ppermute | solution.py:13
  175.5 201.2 %all-reduce.10.cloned.1.call-start = ((), (), s32[]{:S(2)}) async-start(), calls=%async_computation.2 | async-start | bytes 131072 | tf_op jit(solution)/shard_map/psum | solution.py:39
  274.8 55.8 %collective-permute-start.1 = (f32[4096,128]{0,1:T(8,128)S(1)}, f32[4096,128]{0,1:T(8,128)S(1)}, u32[]{:S(2)}, u32[]{:S(2)}) collective-permute-start(f32[4096,128]{0,1:T(8,128)S(1)} %maximum_select_fusion.4), channel_id=1, source_target_pairs={{0,4},{4,8},{8,12},{12,16},{16,20},{20,24},{24,28},{28,32},{32,36}... | collective-permute-start | bytes 6291464 | tf_op jit(solution)/shard_map/ppermute | solution.py:13
  330.8 1.0 copy-start.2
  334.4 201.2 %all-reduce.12.cloned.1.call-start = ((), (), s32[]{:S(2)}) async-start(), calls=%async_computation.3 | async-start | bytes 131072 | tf_op jit(solution)/shard_map/psum | solution.py:39
  433.8 55.8 %collective-permute-start.2 = (f32[4096,128]{0,1:T(8,128)S(1)}, f32[4096,128]{0,1:T(8,128)S(1)}, u32[]{:S(2)}, u32[]{:S(2)}) collective-permute-start(f32[4096,128]{0,1:T(8,128)S(1)} %maximum_select_fusion.8), channel_id=1, source_target_pairs={{0,4},{4,8},{8,12},{12,16},{16,20},{20,24},{24,28},{28,32},{32,36}... | collective-permute-start | bytes 6291464 | tf_op jit(solution)/shard_map/ppermute | solution.py:13
  489.8 1.0 copy-start.3
  593.4 3.5 copy-start.5
  593.5 4.1 copy-start.6
  593.5 4.8 copy-start.7
  593.5 5.5 copy-start.8
  593.7 351.2 %collective-permute-start.3 = (f32[4096,128]{0,1:T(8,128)S(1)}, f32[4096,128]{0,1:T(8,128)}, u32[]{:S(2)}, u32[]{:S(2)}) collective-permute-start(f32[4096,128]{0,1:T(8,128)S(1)} %maximum_select_fusion.12), channel_id=1, source_target_pairs={{0,4},{4,8},{8,12},{12,16},{16,20},{20,24},{24,28},{28,32},{32,36}... | collective-permute-start | bytes 6291464 | tf_op jit(solution)/shard_map/ppermute | solution.py:13
  947.9 64.2 %copy-start.1 = (bf16[4096,128]{1,0:T(8,128)(2,1)S(1)}, bf16[4096,128]{1,0:T(8,128)(2,1)}, u32[]{:S(2)}) copy-start(bf16[4096,128]{1,0:T(8,128)(2,1)} %param.6) | copy-start | bytes 3145732
Sparse Core Ops, SparseCore 0:
  11.5 52.0 all-reduce.5
  175.6 42.1 all-reduce.7
  334.5 42.1 all-reduce.9
  493.5 42.1 all-reduce.11
where the time goes:
time: 1030 us; the launch traced here: 1020 us
  blocking collectives  399 us (39%)
  waiting for transfers between devices  335 us (33%)
  other arithmetic  194 us (19%)
  matrix products  44.6 us (4%)
  between operations  22.5 us (2%)
  starting transfers between devices  13.4 us (1%)
    psum x1, blocking collectives, on_device(): off_total, diag_total = lax.psum((off_part, diag_part), 'pair')  340 us
    psum x4, waiting for transfers between devices, full_gram(): return lax.psum(inner_product(factor, factor), 'row')  177 us
    ppermute x4, waiting for transfers between devices, from_behind(): return lax.ppermute(value, axis, pairs)  158 us
    another operation x24, other arithmetic, orthonormal(): lower = jnp.linalg.cholesky(square)  99.3 us
    another operation x16, other arithmetic, orthonormal(): return jax.scipy.linalg.solve_triangular(lower, block.T, lower=True).T  84.3 us
    psum x1, blocking collectives, on_device(): column_sq = lax.psum(jnp.sum(factor * factor, axis=0), 'row')  59.3 us
    dot_general x12, matrix products, product(): jnp.dot(left, right, precision=HIGH, preferred_element_type=jnp.float32)  24.2 us
  transfers between devices with their start and end apart: 8, of which 7 were waited for; matrix products, arithmetic and copies ran while one was open for 0% of the time, Pallas kernels for 0%

commit v1 on v0

--- a/solution.py
+++ b/solution.py
@@ -5,6 +5,12 @@
 
 ROUNDS = 4
 HIGH = lax.Precision.HIGHEST
+
+
+def add_all(x, name):
+    parts = lax.all_gather(x, name, axis=0, tiled=False)
+    result = parts.sum(axis=0)
+    return result
 
 
 def from_behind(value, axis, steps):
@@ -36,7 +42,7 @@
 
 
 def full_gram(factor):
-    return lax.psum(inner_product(factor, factor), "row")
+    return add_all(inner_product(factor, factor), "row")
 
 
 def on_device(statistic, initial_basis, moving_slot):

time: 1030 us -> 859 us (0.83)
  waiting for transfers between devices: 335 us -> 158 us
  blocking collectives: 399 us -> 431 us
  matrix products: 44.6 us -> 31.3 us
  between operations: 22.5 us -> 9.37 us
    psum x4 -> x0, waiting for transfers between devices: 177 us -> none  [full_gram(): return lax.psum(inner_product(factor, factor), 'row')]
    all_gather x0 -> x4, blocking collectives: none -> 33.4 us  [add_all(): parts = lax.all_gather(x, name, axis=0, tiled=False)]
  transfers between devices with their start and end apart: 8 -> 4, of which waited for: 7 -> 3; matrix products, arithmetic and copies ran while one was open for 0% -> 0% of each run, Pallas kernels for 0% -> 0%
where the time goes in v1:
time: 859 us; the launch traced here: 849 us
  blocking collectives  431 us (50%)
  other arithmetic  203 us (24%)
  waiting for transfers between devices  158 us (18%)
  matrix products  31.3 us (4%)
  between operations  9.37 us (1%)
    psum x1, blocking collectives, on_device(): off_total, diag_total = lax.psum((off_part, diag_part), 'pair')  337 us
    ppermute x4, waiting for transfers between devices, from_behind(): return lax.ppermute(value, axis, pairs)  158 us
    another operation x24, other arithmetic, orthonormal(): lower = jnp.linalg.cholesky(square)  102 us
    another operation x16, other arithmetic, orthonormal(): return jax.scipy.linalg.solve_triangular(lower, block.T, lower=True).T  86 us
    psum x1, blocking collectives, on_device(): column_sq = lax.psum(jnp.sum(factor * factor, axis=0), 'row')  60.1 us
    all_gather x4, blocking collectives, add_all(): parts = lax.all_gather(x, name, axis=0, tiled=False)  33.4 us
    dot_general x12, matrix products, product(): jnp.dot(left, right, precision=HIGH, preferred_element_type=jnp.float32)  20.3 us
  transfers between devices with their start and end apart: 4, of which 3 were waited for; matrix products, arithmetic and copies ran while one was open for 0% of the time, Pallas kernels for 0%

profile of v1, /device:TPU:1, one launch (start us, length us, event | category | flops | bytes accessed | tf_op | source)
XLA Modules:
  0.0 848.9 jit_solution(10887585475683206478)
XLA Ops:
  0.6 1.5 fusion.110
  2.6 12.5 %all-gather = f32[512,128]{1,0:T(8,128)S(1)} all-gather(f32[128,128]{1,0:T(8,128)S(1)} %fusion.111), channel_id=2, replica_groups=mesh['pair'=128,'row'=4] {'row'}, dimensions={0}, use_global_device_ids=true | all-gather | bytes 327680 | tf_op jit(solution)/shard_map/all_gather | solution.py:11
  15.5 11.7 %cholesky.134 = f32[128,128]{1,0:T(8,128)S(1)} custom-call(f32[128,128]{1,0:T(8,128)S(1)} %fusion.74), custom_call_target="Cholesky" | custom-call | tf_op jit(solution)/shard_map/jit(cholesky)/cholesky | solution.py:34
  28.6 9.8 %custom-call.12 = f32[1,128,128]{1,2,0:T(8,128)S(1)} custom-call(f32[1,128,128]{2,1,0:T(8,128)S(1)} %fusion.35), custom_call_target="InvertDiagBlocksLowerTriangular" | custom-call | tf_op jit(solution)/shard_map/jit(_solve_triangular)/triangular_solve | solution.py:35
  39.4 11.7 %cholesky.145 = f32[128,128]{1,0:T(8,128)S(1)} custom-call(f32[128,128]{1,0:T(8,128)S(1)} %fusion.70), custom_call_target="Cholesky" | custom-call | tf_op jit(solution)/shard_map/jit(cholesky)/cholesky | solution.py:34
  52.4 10.0 %custom-call.13 = f32[1,128,128]{1,2,0:T(8,128)S(1)} custom-call(f32[1,128,128]{2,1,0:T(8,128)S(1)} %fusion.36), custom_call_target="InvertDiagBlocksLowerTriangular" | custom-call | tf_op jit(solution)/shard_map/jit(_solve_triangular)/triangular_solve | solution.py:35
  62.7 1.0 convolution_bitcast_fusion.1
  63.7 1.0 convolution_bitcast_fusion
  66.3 1.9 collective-permute-start
  68.9 54.0 %collective-permute-done = f32[4096,128]{0,1:T(8,128)S(1)} collective-permute-done((f32[4096,128]{0,1:T(8,128)S(1)}, f32[4096,128]{0,1:T(8,128)S(1)}, u32[]{:S(2)}, u32[]{:S(2)}) %collective-permute-start) | collective-permute-done | bytes 2097184 | tf_op jit(solution)/shard_map/ppermute | solution.py:19
  123.0 2.0 fusion.25
  125.1 6.3 all-gather.1
  131.8 11.7 %cholesky.156 = f32[128,128]{1,0:T(8,128)S(1)} custom-call(f32[128,128]{1,0:T(8,128)S(1)} %fusion.66), custom_call_target="Cholesky" | custom-call | tf_op jit(solution)/shard_map/jit(cholesky)/cholesky | solution.py:34
  144.8 9.8 %custom-call.14 = f32[1,128,128]{1,2,0:T(8,128)S(1)} custom-call(f32[1,128,128]{2,1,0:T(8,128)S(1)} %fusion.37), custom_call_target="InvertDiagBlocksLowerTriangular" | custom-call | tf_op jit(solution)/shard_map/jit(_solve_triangular)/triangular_solve | solution.py:35
  155.6 11.7 %cholesky.167 = f32[128,128]{1,0:T(8,128)S(1)} custom-call(f32[128,128]{1,0:T(8,128)S(1)} %fusion.62), custom_call_target="Cholesky" | custom-call | tf_op jit(solution)/shard_map/jit(cholesky)/cholesky | solution.py:34
  168.7 10.2 %custom-call.15 = f32[1,128,128]{1,2,0:T(8,128)S(1)} custom-call(f32[1,128,128]{2,1,0:T(8,128)S(1)} %fusion.38), custom_call_target="InvertDiagBlocksLowerTriangular" | custom-call | tf_op jit(solution)/shard_map/jit(_solve_triangular)/triangular_solve | solution.py:35
  179.1 3.7 fusion.24
  182.8 2.1 fusion
  185.9 1.9 collective-permute-start.1
  188.5 52.1 %collective-permute-done.1 = f32[4096,128]{0,1:T(8,128)S(1)} collective-permute-done((f32[4096,128]{0,1:T(8,128)S(1)}, f32[4096,128]{0,1:T(8,128)S(1)}, u32[]{:S(2)}, u32[]{:S(2)}) %collective-permute-start.1) | collective-permute-done | bytes 2097184 | tf_op jit(solution)/shard_map/ppermute | solution.py:19
  240.8 2.0 fusion.23
  242.8 7.2 all-gather.2
  251.4 11.7 %cholesky.178 = f32[128,128]{1,0:T(8,128)S(1)} custom-call(f32[128,128]{1,0:T(8,128)S(1)} %fusion.58), custom_call_target="Cholesky" | custom-call | tf_op jit(solution)/shard_map/jit(cholesky)/cholesky | solution.py:34
  264.4 9.8 %custom-call.16 = f32[1,128,128]{1,2,0:T(8,128)S(1)} custom-call(f32[1,128,128]{2,1,0:T(8,128)S(1)} %fusion.39), custom_call_target="InvertDiagBlocksLowerTriangular" | custom-call | tf_op jit(solution)/shard_map/jit(_solve_triangular)/triangular_solve | solution.py:35
  275.8 12.5 %cholesky.189 = f32[128,128]{1,0:T(8,128)S(1)} custom-call(f32[128,128]{1,0:T(8,128)} %fusion.54), custom_call_target="Cholesky" | custom-call | tf_op jit(solution)/shard_map/jit(cholesky)/cholesky | solution.py:34
  289.7 10.0 %custom-call.17 = f32[1,128,128]{1,2,0:T(8,128)S(1)} custom-call(f32[1,128,128]{2,1,0:T(8,128)S(1)} %fusion.40), custom_call_target="InvertDiagBlocksLowerTriangular" | custom-call | tf_op jit(solution)/shard_map/jit(_solve_triangular)/triangular_solve | solution.py:35
  300.0 3.7 fusion.22
  303.7 2.1 fusion.6
  306.7 1.9 collective-permute-start.2
  309.3 52.1 %collective-permute-done.2 = f32[4096,128]{0,1:T(8,128)S(1)} collective-permute-done((f32[4096,128]{0,1:T(8,128)S(1)}, f32[4096,128]{0,1:T(8,128)S(1)}, u32[]{:S(2)}, u32[]{:S(2)}) %collective-permute-start.2) | collective-permute-done | bytes 2097184 | tf_op jit(solution)/shard_map/ppermute | solution.py:19
  361.6 2.0 fusion.21
  363.6 7.4 all-gather.3
  371.1 1.0 reduce_sum.120
  373.1 12.5 %cholesky.200 = f32[128,128]{1,0:T(8,128)S(1)} custom-call(f32[128,128]{1,0:T(8,128)} %fusion.50), custom_call_target="Cholesky" | custom-call | tf_op jit(solution)/shard_map/jit(cholesky)/cholesky | solution.py:34
  387.0 9.8 %custom-call.18 = f32[1,128,128]{1,2,0:T(8,128)S(1)} custom-call(f32[1,128,128]{2,1,0:T(8,128)S(1)} %fusion.41), custom_call_target="InvertDiagBlocksLowerTriangular" | custom-call | tf_op jit(solution)/shard_map/jit(_solve_triangular)/triangular_solve | solution.py:35
  398.3 1.5 fusion.46
  399.8 12.5 %cholesky.211 = f32[128,128]{1,0:T(8,128)S(1)} custom-call(f32[128,128]{1,0:T(8,128)} %fusion.46), custom_call_target="Cholesky" | custom-call | tf_op jit(solution)/shard_map/jit(cholesky)/cholesky | solution.py:34
  413.0 1.3 fusion.42
  414.3 10.8 %custom-call.19 = f32[1,128,128]{1,2,0:T(8,128)S(1)} custom-call(f32[1,128,128]{2,1,0:T(8,128)} %fusion.42), custom_call_target="InvertDiagBlocksLowerTriangular" | custom-call | tf_op jit(solution)/shard_map/jit(_solve_triangular)/triangular_solve | solution.py:35
  425.4 3.6 fusion.20
  429.1 2.1 fusion.12
  431.2 1.3 broadcast_select_fusion
  433.1 1.9 collective-permute-start.3
  437.7 337.5 %all-reduce = (f32[]{:T(128)}, f32[]{:T(128)}, f32[]{:T(128)}, f32[]{:T(128)}, f32[]{:T(128)}, /*index=5*/f32[]{:T(128)}, f32[]{:T(128)}, f32[]{:T(128)}) all-reduce(f32[]{:T(128)} %get-tuple-element.18, f32[]{:T(128)} %get-tuple-element.17, f32[]{:T(128)} %get-tuple-element.16, ...), channel_id=1, replica_groups=mesh['pair'=128,'row'=4] {'pair'}, use_global_device_ids=true, to_apply=%region_21.24 | all-reduce | flops 8 | bytes 64 | tf_op jit(solution)/shard_map/psum | solution.py:60
  781.0 2.7 fusion.102
  783.9 1.8 copy.23
  785.7 2.5 fusion.19
  788.1 60.1 %psum.63 = f32[128]{0:T(128)S(1)} all-reduce(f32[128]{0:T(128)S(1)} %fusion.19), channel_id=1, replica_groups=mesh['pair'=128,'row'=4] {'row'}, use_global_device_ids=true, to_apply=%region_7.10 | all-reduce | flops 128 | bytes 1024 | tf_op jit(solution)/shard_map/psum | solution.py:89
  (95 shorter events, 27.7 us)
Async XLA Ops:
  0.6 1.5 copy-start
  39.0 24.8 %copy-start.5 = (bf16[4096,128]{1,0:T(8,128)(2,1)S(1)}, bf16[4096,128]{1,0:T(8,128)(2,1)}, u32[]{:S(2)}) copy-start(bf16[4096,128]{1,0:T(8,128)(2,1)} %param.7) | copy-start | bytes 3145732
  66.0 57.1 %copy-start.4 = (f32[4096,64]{0,1:T(8,128)}, f32[4096,64]{0,1:T(8,128)S(1)}, u32[]{:S(2)}) copy-start(f32[4096,64]{0,1:T(8,128)S(1)} %get-tuple-element.64) | copy-start | bytes 3145732
  66.3 56.6 %collective-permute-start = (f32[4096,128]{0,1:T(8,128)S(1)}, f32[4096,128]{0,1:T(8,128)S(1)}, u32[]{:S(2)}, u32[]{:S(2)}) collective-permute-start(f32[4096,128]{0,1:T(8,128)S(1)} %maximum_select_fusion), channel_id=1, source_target_pairs={{0,4},{4,8},{8,12},{12,16},{16,20},{20,24},{24,28},{28,32},{32,36}... | collective-permute-start | bytes 6291464 | tf_op jit(solution)/shard_map/ppermute | solution.py:19
  185.9 54.7 %collective-permute-start.1 = (f32[4096,128]{0,1:T(8,128)S(1)}, f32[4096,128]{0,1:T(8,128)S(1)}, u32[]{:S(2)}, u32[]{:S(2)}) collective-permute-start(f32[4096,128]{0,1:T(8,128)S(1)} %maximum_select_fusion.4), channel_id=1, source_target_pairs={{0,4},{4,8},{8,12},{12,16},{16,20},{20,24},{24,28},{28,32},{32,36}... | collective-permute-start | bytes 6291464 | tf_op jit(solution)/shard_map/ppermute | solution.py:19
  240.8 2.0 copy-start.3
  306.7 54.7 %collective-permute-start.2 = (f32[4096,128]{0,1:T(8,128)S(1)}, f32[4096,128]{0,1:T(8,128)S(1)}, u32[]{:S(2)}, u32[]{:S(2)}) collective-permute-start(f32[4096,128]{0,1:T(8,128)S(1)} %maximum_select_fusion.8), channel_id=1, source_target_pairs={{0,4},{4,8},{8,12},{12,16},{16,20},{20,24},{24,28},{28,32},{32,36}... | collective-permute-start | bytes 6291464 | tf_op jit(solution)/shard_map/ppermute | solution.py:19
  361.6 2.0 copy-start.2
  433.1 347.9 %collective-permute-start.3 = (f32[4096,128]{0,1:T(8,128)S(1)}, f32[4096,128]{0,1:T(8,128)}, u32[]{:S(2)}, u32[]{:S(2)}) collective-permute-start(f32[4096,128]{0,1:T(8,128)S(1)} %maximum_select_fusion.12), channel_id=1, source_target_pairs={{0,4},{4,8},{8,12},{12,16},{16,20},{20,24},{24,28},{28,32},{32,36}... | collective-permute-start | bytes 6291464 | tf_op jit(solution)/shard_map/ppermute | solution.py:19
  783.8 64.9 %copy-start.1 = (bf16[4096,128]{1,0:T(8,128)(2,1)S(1)}, bf16[4096,128]{1,0:T(8,128)(2,1)}, u32[]{:S(2)}) copy-start(bf16[4096,128]{1,0:T(8,128)(2,1)} %param.6) | copy-start | bytes 3145732
